TPU v7x, 256 devices: a whole 4x4x8 slice. The times are simulated.
256 devices in a mesh: rows: 64 (over z, x, core), feat: 4 (over y).
Axes of the slice: x: 4, y: 4, z: 8, core: 2. Of those that a mesh axis runs over, the one named last changes fastest.
Arguments:
- feats: bfloat16 [256, 262144], P('feat', 'rows'), may hold values from -6 to 6
- weight: bfloat16 [256, 256], replicated, may hold values from -0.375 to 0.375
- hub_adj: bfloat16 [262144, 512], P('rows'), may hold values from -0.75 to 0.75
- hub_rows: int32 [512], P('rows'), may hold values from 0 to 4095, as said below
- send_cols: int32 [64, 64, 128], P('rows'), may hold values from 0 to 4095
- send_counts: int32 [64, 64], P('rows'), may hold values from 8 to 128, as said below
- tile_cols: int32 [2048, 4], P('rows'), may hold values from 0 to 63, all different within a row
- tile_vals: bfloat16 [2048, 4, 128, 128], P('rows'), may hold values from -0.25 to 0.25
- cot: bfloat16 [256, 262144], P('feat', 'rows'), may hold values from -6 to 6
Outputs:
- out: bfloat16 [256, 262144], P('feat', 'rows')
- grad_feats: float32 [256, 262144], P('feat', 'rows')
- grad_weight: float32 [256, 256], P(None, 'feat')
Inputs may be any that keep to these rules, and one draw needn't show every extreme that they name: `hub_rows`: the 8 entries of one owner are distinct rows of its block. `send_cols`: entries past send_counts are ignored; a list may repeat a row. `send_counts`: in every draw some destination receives 128 rows from every sender. `tile_cols`: the 4 senders of one destination block are distinct.
All inputs are finite; a program needn't handle non-finite values.
Results may differ from a plain program's by a relative error of at most 0.0056.
Values may be sent and summed in bfloat16 or wider, within the bound.
A program may use at most 64 MiB of HBM per device.

v0:
```python
import math

import jax
import jax.numpy as jnp
from jax import lax
from jax.sharding import PartitionSpec as P


def on_device(feats, weight, hub_adj, hub_rows, send_cols, send_counts, tile_cols, tile_vals, cot):
    feat_dev = feats.shape[0]
    row_count = feats.shape[1]
    peer_count = send_cols.shape[1]
    capacity = send_cols.shape[2]
    block_count = tile_cols.shape[0]
    tile_count = tile_cols.shape[1]
    block_rows = tile_vals.shape[2]
    feat_start = lax.axis_index("feat") * feat_dev
    own_hubs = feats[:, hub_rows]
    empty = jnp.zeros((feat_dev, row_count), jnp.float32)
    hub_part = lax.dot_general(
        lax.all_gather(own_hubs, "rows", axis=1, tiled=True),
        hub_adj,
        (((1,), (1,)), ((), ())),
        preferred_element_type=jnp.float32,
    )
    live = (jnp.arange(capacity, dtype=jnp.int32)[None, :] < send_counts[0][:, None]).reshape(-1)
    flat_cols = send_cols[0].reshape(-1)
    outgoing = jnp.where(live[None, :], feats[:, flat_cols], jnp.zeros((), jnp.bfloat16))
    incoming = lax.all_to_all(outgoing, "rows", split_axis=1, concat_axis=1, tiled=True)
    picked = incoming.reshape(feat_dev, peer_count, capacity)[:, tile_cols]
    ragged = jnp.einsum("fbtc,btic->fbi", picked, tile_vals, preferred_element_type=jnp.float32)
    agg = (hub_part + ragged.reshape(feat_dev, row_count)).astype(jnp.bfloat16)
    own_cols = lax.dynamic_slice_in_dim(weight, feat_start, feat_dev, 1)
    agg_full = lax.all_gather(agg, "feat", axis=0, tiled=True)
    pre = lax.dot_general(
        own_cols, agg_full, (((0,), (0,)), ((), ())), preferred_element_type=jnp.float32
    )
    out = jax.nn.silu(pre).astype(jnp.bfloat16)
    sigma = jax.nn.sigmoid(pre)
    slope = (cot.astype(jnp.float32) * (sigma * (1.0 + pre * (1.0 - sigma)))).astype(jnp.bfloat16)
    weight_terms = lax.dot_general(
        agg_full, slope, (((1,), (1,)), ((), ())), preferred_element_type=jnp.float32
    )
    node_total = row_count * lax.axis_size("rows")
    grad_weight = lax.psum(weight_terms, "rows") * (1.0 / math.sqrt(node_total))
    grad_agg = lax.psum_scatter(
        jnp.dot(own_cols, slope, preferred_element_type=jnp.float32),
        "feat",
        scatter_dimension=0,
        tiled=True,
    ).astype(jnp.bfloat16)
    hub_terms = jnp.dot(grad_agg, hub_adj, preferred_element_type=jnp.float32)
    own_hub_grad = lax.psum_scatter(hub_terms, "rows", scatter_dimension=1, tiled=True)
    grad_feats = empty.at[:, hub_rows].add(own_hub_grad)
    grad_blocks = grad_agg.reshape(feat_dev, block_count, block_rows)
    per_tile = jnp.einsum(
        "fbi,btic->fbtc", grad_blocks, tile_vals, preferred_element_type=jnp.float32
    )
    per_tile = per_tile.reshape(feat_dev, block_count * tile_count, capacity)
    selector = (
        tile_cols.reshape(-1)[:, None] == jnp.arange(peer_count, dtype=jnp.int32)[None, :]
    ).astype(jnp.float32)
    back = jnp.einsum("fkc,kn->fnc", per_tile, selector, precision=lax.Precision.HIGHEST)
    returned = lax.all_to_all(
        back.reshape(feat_dev, peer_count * capacity).astype(jnp.bfloat16),
        "rows",
        split_axis=1,
        concat_axis=1,
        tiled=True,
    ).astype(jnp.float32)
    returned = jnp.where(live[None, :], returned, jnp.zeros((), jnp.float32))
    grad_feats = grad_feats.at[:, flat_cols].add(returned)
    return (out, grad_feats, grad_weight)


def solution(mesh):
    in_specs = (
        P("feat", "rows"),
        P(),
        P("rows", None),
        P("rows"),
        P("rows", None, None),
        P("rows", None),
        P("rows", None),
        P("rows", None, None, None),
        P("feat", "rows"),
    )
    out_specs = (P("feat", "rows"), P("feat", "rows"), P(None, "feat"))
    return jax.shard_map(
        on_device, mesh=mesh, in_specs=in_specs, out_specs=out_specs, check_vma=False
    )
```

profile of v0, /device:TPU:1, one launch (start us, length us, event | category | flops | bytes accessed | tf_op | source)
XLA Modules:
  0.0 484.3 jit_solution(1300707965968538869)
XLA Ops:
  7.2 0.0 copy-start
  7.2 0.8 fusion.25
  8.0 0.8 compare_select_fusion
  8.8 1.5 copy.42
  10.3 24.0 %gather_fusion.1 = bf16[8192,64]{1,0:T(8,128)(2,1)S(1)} fusion(bf16[64,4096]{0,1:T(8,128)(2,1)S(1)} %copy.42, s32[8192]{0:T(1024)S(1)} %broadcast_clamp_fusion), kind=kCustom, calls=%fused_computation.1 | custom fusion | bytes 2129920 | tf_op jit(solution)/shard_map/gather | solution.py:28
  34.3 1.6 copy.44
  36.0 2.3 broadcast_select_fusion
  38.3 13.0 %all-to-all-start = ((bf16[64,64,128]{2,0,1:T(8,128)(2,1)}), bf16[64,64,128]{2,0,1:T(8,128)(2,1)S(1)}, u32[]{:S(2)}, u32[]{:S(2)}) async-start(bf16[64,64,128]{2,0,1:T(8,128)(2,1)} %broadcast_select_fusion), calls=%async_computation | async-start | bytes 2097152 | tf_op jit(solution)/shard_map/all_to_all | solution.py:29
  51.3 0.0 all-gather.3.cloned.1.call-start
  51.3 0.1 copy.45
  51.4 0.1 reshape.96
  51.6 0.6 gather_fusion
  52.1 67.4 %all-gather = bf16[64,512]{0,1:T(8,128)(2,1)S(1)} all-gather(bf16[64,8]{0,1:T(8,128)(2,1)S(1)} %bitcast.62), channel_id=2, replica_groups=mesh['rows'=64,'feat'=4] {'rows'}, dimensions={1}, use_global_device_ids=true | all-gather | bytes 66560 | tf_op jit(solution)/shard_map/all_gather | solution.py:21
  119.5 0.0 all-to-all-done
  119.5 2.1 gather_fusion.2
  121.6 4.5 convolution_bitcast_fusion
  126.2 0.0 copy-start.5
  126.2 2.2 fusion
  128.4 0.0 all-gather.3.cloned.1.call-update
  128.4 0.2 reduce-scatter.2.cloned.1.call-start
  128.6 32.9 %all-gather.3.cloned.1.call-done = bf16[256,4096]{1,0:T(8,128)(2,1)} async-done(((bf16[64,4096]{1,0:T(8,128)(2,1)}), bf16[256,4096]{1,0:T(8,128)(2,1)}) %all-gather.3.cloned.1.call-update) | async-done | bytes 2097168 | tf_op jit(solution)/shard_map/all_gather | solution.py:34
  161.5 0.0 copy-done.5
  161.5 3.2 multiply_convert_fusion
  164.7 2.7 fusion.16
  167.4 0.0 reduce-scatter.2.cloned.1.call-update
  167.5 0.1 copy.47
  167.5 0.1 eq.15
  167.7 49.4 %reduce-scatter.2.cloned.1.call-done = f32[64,4096]{1,0:T(8,128)} async-done(((f32[256,4096]{1,0:T(8,128)}), f32[64,4096]{1,0:T(8,128)}) %reduce-scatter.2.cloned.1.call-update) | async-done | bytes 1048592 | tf_op jit(solution)/shard_map/reduce_scatter | solution.py:46
  217.1 1.3 convert_bitcast_fusion.1
  218.4 0.1 copy.60
  218.5 3.0 fusion.12
  221.5 4.1 fusion.7
  225.6 1.6 copy.50
  227.3 10.7 %all-to-all-start.1 = ((bf16[64,64,128]{2,0,1:T(8,128)(2,1)}), bf16[64,64,128]{2,0,1:T(8,128)(2,1)S(1)}, u32[]{:S(2)}, u32[]{:S(2)}) async-start(bf16[64,64,128]{2,0,1:T(8,128)(2,1)} %copy.50), calls=%async_computation.2 | async-start | bytes 2097152 | tf_op jit(solution)/shard_map/all_to_all | solution.py:64
  238.0 0.0 all-reduce.4.cloned.1.call-start
  238.1 3.0 fusion.26
  241.0 0.0 copy-done.2
  241.1 4.6 fusion.14
  245.7 0.0 all-reduce.4.cloned.1.call-update
  245.7 0.6 dynamic-slice
  247.0 176.9 %all-reduce.4.cloned.1.call-done = (f32[64,512]{0,1:T(8,128)}, f32[256,64]{0,1:T(8,128)}) async-done(((f32[64,512]{0,1:T(8,128)}, f32[256,64]{0,1:T(8,128)}), (f32[64,512]{0,1:T(8,128)}, f32[256,64]{0,1:T(8,128)})) %all-reduce.4.cloned.1.call-update) | async-done | bytes 196624
  423.9 1.3 scatter_custom_fusion
  425.2 0.6 broadcast_multiply_fusion
  425.8 0.0 all-to-all-done.1
  425.8 1.5 fusion.3
  427.3 3.8 copy.52
  431.1 45.1 %scatter_fusion = f32[64,4096]{0,1:T(8,128)S(1)} fusion(f32[64,4096]{0,1:T(8,128)S(1)} %scatter_custom_fusion, s32[8192]{0:T(1024)S(1)} %bitcast.61, f32[8192,64]{1,0:T(8,128)} %copy.52), kind=kCustom, calls=%fused_computation.4 | custom fusion | flops 524288 | bytes 6324224 | tf_op jit(solution)/shard_map/scatter-add | solution.py:72
  476.2 1.6 copy.53
  (17 shorter events, 0.0 us)
Async XLA Ops:
  7.2 154.3 %copy-start = (bf16[256,256]{1,0:T(8,128)(2,1)S(1)}, bf16[256,256]{1,0:T(8,128)(2,1)}, u32[]{:S(2)}) copy-start(bf16[256,256]{1,0:T(8,128)(2,1)} %param.10) | copy-start | bytes 393220
  35.9 15.4 %copy-start.4 = (s32[32,4]{0,1:T(4,128)S(1)}, s32[32,4]{0,1:T(4,128)}, u32[]{:S(2)}) copy-start(s32[32,4]{0,1:T(4,128)} %param.15) | copy-start | bytes 1540
  36.0 15.6 %copy-start.6 = (s32[8]{0:T(128)S(1)}, s32[8]{0:T(128)}, u32[]{:S(2)}) copy-start(s32[8]{0:T(128)} %param.12) | copy-start | bytes 100
  38.3 81.2 %all-to-all-start = ((bf16[64,64,128]{2,0,1:T(8,128)(2,1)}), bf16[64,64,128]{2,0,1:T(8,128)(2,1)S(1)}, u32[]{:S(2)}, u32[]{:S(2)}) async-start(bf16[64,64,128]{2,0,1:T(8,128)(2,1)} %broadcast_select_fusion), calls=%async_computation | async-start | bytes 2097152 | tf_op jit(solution)/shard_map/all_to_all | solution.py:29
  51.3 110.2 %all-gather.3.cloned.1.call-start = ((), (), s32[]{:S(2)}) async-start(), calls=%async_computation.3 | async-start | bytes 2621440 | tf_op jit(solution)/shard_map/all_gather | solution.py:34
  121.6 4.5 copy-start.1
  126.2 35.4 %copy-start.5 = (bf16[64,4096]{1,0:T(8,128)(2,1)S(1)}, bf16[64,4096]{1,0:T(8,128)(2,1)}, u32[]{:S(2)}) copy-start(bf16[64,4096]{1,0:T(8,128)(2,1)} %param.17) | copy-start | bytes 1572868
  128.4 88.7 %reduce-scatter.2.cloned.1.call-start = ((), (), s32[]{:S(2)}) async-start(), calls=%async_computation.4 | async-start | bytes 5242880 | tf_op jit(solution)/shard_map/reduce_scatter | solution.py:46
  227.3 13.8 %copy-start.2 = (f32[64,4096]{1,0:T(8,128)S(1)}, f32[64,4096]{1,0:T(8,128)}, u32[]{:S(2)}) copy-start(f32[64,4096]{1,0:T(8,128)} %reduce-scatter.2.cloned.1.call-done) | copy-start | bytes 3145732
  227.3 198.6 %all-to-all-start.1 = ((bf16[64,64,128]{2,0,1:T(8,128)(2,1)}), bf16[64,64,128]{2,0,1:T(8,128)(2,1)S(1)}, u32[]{:S(2)}, u32[]{:S(2)}) async-start(bf16[64,64,128]{2,0,1:T(8,128)(2,1)} %copy.50), calls=%async_computation.2 | async-start | bytes 2097152 | tf_op jit(solution)/shard_map/all_to_all | solution.py:64
  238.0 185.9 %all-reduce.4.cloned.1.call-start = ((), (), s32[]{:S(2)}) async-start(), calls=%async_computation.5 | async-start | bytes 655360
  241.0 4.7 copy-start.7
  423.9 1.3 copy-start.3
Sparse Core Ops, SparseCore 0:
  128.5 32.9 all-gather.2
  167.6 49.4 reduce-scatter.1
  245.8 178.0 all-reduce.3
where the time goes:
time: 485 us; the launch traced here: 484 us
  waiting for transfers between devices  259 us (53%)
  blocking collectives  67.4 us (14%)
  other arithmetic  53.7 us (11%)
  local copies, waits for them, and re-layouts  38 us (8%)
  matrix products  27.3 us (6%)
  starting transfers between devices  24 us (5%)
  between operations  14.6 us (3%)
    unnamed x4, waiting for transfers between devices  177 us
    all_gather x1, blocking collectives, on_device(): lax.all_gather(own_hubs, 'rows', axis=1, tiled=True)  67.4 us
    reduce_scatter x1, waiting for transfers between devices, on_device(): lax.psum_scatter(jnp.dot(own_cols, slope, preferred_element_type=jnp.floa...  49.4 us
    scatter-add x1, other arithmetic, on_device(): grad_feats = grad_feats.at[:, flat_cols].add(returned)  45.1 us
    all_gather x1, waiting for transfers between devices, on_device(): agg_full = lax.all_gather(agg, 'feat', axis=0, tiled=True)  32.9 us
    gather x2, local copies, waits for them, and re-layouts, on_device(): feats[:, flat_cols]  25.7 us
    all_to_all x1, starting transfers between devices, on_device(): lax.all_to_all(outgoing, 'rows', split_axis=1, concat_axis=1, tiled=True)  13 us
    all_to_all x1, starting transfers between devices, on_device(): lax.all_to_all(back.reshape(feat_dev, peer_count * capacity).astype(jnp.b...  10.7 us
  transfers between devices with their start and end apart: 5, of which 3 were waited for; matrix products, arithmetic and copies ran while one was open for 2% of the time, Pallas kernels for 0%

commit v1 on v0

v1 whole, which is shorter than its diff:
```python
import functools
import math

import jax
import jax.numpy as jnp
from jax import lax
from jax.experimental import pallas as pl
from jax.experimental.pallas import tpu as pltpu
from jax.sharding import PartitionSpec as P

MESH = pl.DeviceIdType.MESH
F32 = jnp.float32
BF16 = jnp.bfloat16
NN = (((1,), (0,)), ((), ()))
NT = (((1,), (1,)), ((), ()))
TN = (((0,), (0,)), ((), ()))
EARLY = 12


def dot(a, b, dims=NN):
    return lax.dot_general(a, b, dims, preferred_element_type=F32)


def layer_kernel(
    feats, weight, hadj_hbm, hubrows, cols, tv_hbm, cot, sm,
    out, gfeats, gweight,
    hadj, tv, feat_hi, onehot_hub, hub_own, hub_z, hub_zb, hub_xc, hub_t, hub_acc,
    send, recv, agg_send, agg_full, cot_full, slopes, outs, gas, ga, chain, bsend, brecv,
    scat, wt, w_y, w_1, w_xc, w_2, w_z, w_3, w_4, h_1, h_xc, h_2, h_z,
    lsem, a_s, a_r, b_s, b_r, hz_s, hz_r, hx_s, hx_r, c_s, c_r, y_s, y_r, g_s, g_r, o_s, o_r,
    wy_s, wy_r, wx_s, wx_r, wz_s, wz_r, w4_s, w4_r, h1_s, h1_r, h2_s, h2_r,
):
    me = lax.axis_index("rows")
    y = lax.axis_index("feat")
    z = lax.div(me, 8)
    xc = lax.rem(me, 8)
    x = lax.div(xc, 2)
    c = lax.rem(xc, 2)

    def dest(k):
        return (
            lax.rem(z + 1 + lax.rem(k, 8), 8) * 8
            + lax.rem(x + 1 + lax.div(k, 16), 4) * 2
            + lax.rem(c + 1 + lax.rem(lax.div(k, 8), 2), 2)
        )

    def source(k):
        return (
            lax.rem(z + 7 - lax.rem(k, 8), 8) * 8
            + lax.rem(x + 3 - lax.div(k, 16), 4) * 2
            + lax.rem(c + 1 + lax.rem(lax.div(k, 8), 2), 2)
        )

    def z_peer(m):
        return lax.rem(z + m, 8)

    def xc_peer(m):
        return lax.rem(xc + m, 8)

    def y_peer(m):
        return lax.rem(y + m, 4)

    def to_rows(src, dst, ssem, rsem, peer):
        return pltpu.make_async_remote_copy(
            src_ref=src, dst_ref=dst, send_sem=ssem, recv_sem=rsem,
            device_id={"rows": peer}, device_id_type=MESH,
        )

    def to_feat(src, dst, ssem, rsem, peer):
        return pltpu.make_async_remote_copy(
            src_ref=src, dst_ref=dst, send_sem=ssem, recv_sem=rsem,
            device_id={"feat": peer}, device_id_type=MESH,
        )

    barrier = pltpu.get_barrier_semaphore()

    @pl.loop(1, 64)
    def _(k):
        pl.semaphore_signal(
            barrier, inc=1, device_id={"rows": lax.rem(me + k, 64)}, device_id_type=MESH
        )

    for m in range(1, 4):
        pl.semaphore_signal(barrier, inc=1, device_id={"feat": y_peer(m)}, device_id_type=MESH)
    load_tv = pltpu.make_async_copy(tv_hbm, tv, lsem.at[0])
    load_hadj = pltpu.make_async_copy(hadj_hbm, hadj, lsem.at[1])
    load_hadj.start()
    load_tv.start()

    for hi in range(8):
        feat_hi[pl.ds(hi * 64, 64), :] = feats[:, pl.ds(hi * 512, 512)]
    row_at = lax.broadcasted_iota(jnp.int32, (16, 4096), 1)
    onehot_hub[...] = jnp.where(row_at == hubrows[...], 1.0, 0.0).astype(BF16)
    own = dot(onehot_hub[...], feats[...], NT)
    hub_own[...] = jnp.concatenate([own[:8], jnp.zeros((8, 64), F32)], axis=1)
    chain[0] = jnp.zeros((64, 128), F32)

    def onehot(col, width):
        low = jnp.broadcast_to(jnp.bitwise_and(col, 511), (512, width))
        at = lax.broadcasted_iota(jnp.int32, (512, width), 0)
        return jnp.where(at == low, 1.0, 0.0).astype(BF16)

    def gather(g):
        p0, p1 = dest(2 * g), dest(2 * g + 1)
        col = jnp.concatenate([cols[pl.ds(p0, 1), :], cols[pl.ds(p1, 1), :]], axis=1)
        picked = dot(feat_hi[...], onehot(col, 256))
        high = jnp.broadcast_to(lax.shift_right_arithmetic(col, 9), (64, 256))
        acc = jnp.zeros((64, 256), F32)
        for hi in range(8):
            acc = jnp.where(high == hi, picked[hi * 64 : hi * 64 + 64], acc)
        acc = acc.astype(BF16)
        send[p0] = acc[:, :128]
        send[p1] = acc[:, 128:]

    def forward(k):
        p = dest(k)
        return to_rows(send.at[p], recv.at[me], a_s.at[p], a_r.at[me], p)

    @pl.loop(0, EARLY)
    def _(g):
        gather(g)

    pl.semaphore_wait(barrier, 66)

    def hub_stage1(m):
        p = z_peer(m)
        return to_rows(hub_own, hub_z.at[z], hz_s.at[p], hz_r.at[z], p * 8 + xc)

    def hub_stage1_in(m):
        p = z_peer(m)
        return to_rows(hub_own, hub_z.at[p], hz_s.at[p], hz_r.at[p], p * 8 + xc)

    @pl.loop(1, 8)
    def _(m):
        hub_stage1(m).start()

    hub_z[z] = hub_own[...]

    @pl.loop(0, 2 * EARLY)
    def _(k):
        forward(k).start()

    def cot_out(m):
        p = y_peer(m)
        return to_feat(
            cot.at[:, pl.ds(pl.multiple_of(p * 1024, 1024), 1024)],
            cot_full.at[pl.ds(pl.multiple_of(y * 64, 64), 64)], c_s.at[p], c_r.at[y], p,
        )

    def cot_in(m):
        p = y_peer(m)
        return to_feat(
            cot.at[:, pl.ds(pl.multiple_of(p * 1024, 1024), 1024)],
            cot_full.at[pl.ds(pl.multiple_of(p * 64, 64), 64)], c_s.at[p], c_r.at[p], p,
        )

    for m in (2, 1, 3):
        cot_out(m).start()
    cot_full[pl.ds(pl.multiple_of(y * 64, 64), 64), :] = cot[
        :, pl.ds(pl.multiple_of(y * 1024, 1024), 1024)
    ]

    @pl.loop(EARLY, 31)
    def _(g):
        gather(g)
        forward(2 * g).start()
        forward(2 * g + 1).start()

    gather(jnp.int32(31))
    forward(jnp.int32(62)).start()
    recv[me] = send[me]

    @pl.loop(1, 8)
    def _(m):
        hub_stage1_in(m).wait_recv()

    hub_zb[...] = hub_z[...].reshape(64, 128).astype(BF16)

    def hub_stage2(m):
        p = xc_peer(m)
        return to_rows(hub_zb, hub_xc.at[xc], hx_s.at[p], hx_r.at[xc], z * 8 + p)

    def hub_stage2_in(m):
        p = xc_peer(m)
        return to_rows(hub_zb, hub_xc.at[p], hx_s.at[p], hx_r.at[p], z * 8 + p)

    @pl.loop(1, 8)
    def _(m):
        hub_stage2(m).start()

    hub_xc[xc] = hub_zb[...]
    load_hadj.wait()
    load_tv.wait()

    @pl.loop(1, 8)
    def _(m):
        hub_stage2_in(m).wait_recv()

    for p in range(8):
        part = hub_xc[p].astype(F32)
        for zz in range(8):
            hub_t[pl.ds(zz * 64 + p * 8, 8), :] = part[zz * 8 : zz * 8 + 8]
    hubs = hub_t[...].T[:64].astype(BF16)

    @pl.loop(0, 8)
    def _(n):
        at = pl.ds(pl.multiple_of(n * 512, 512), 512)
        hub_acc[:, at] = dot(hubs, hadj[at, :], NT)

    @pl.loop(0, 63)
    def _(k):
        q = source(k)
        to_rows(send.at[q], recv.at[q], a_s.at[q], a_r.at[q], q).wait_recv()

    def agg_out(m):
        p = y_peer(m)
        return to_feat(
            agg_send.at[p], agg_full.at[pl.ds(pl.multiple_of(y * 64, 64), 64)],
            y_s.at[p], y_r.at[y], p,
        )

    def agg_in(m):
        p = y_peer(m)
        return to_feat(
            agg_send.at[p], agg_full.at[pl.ds(pl.multiple_of(p * 64, 64), 64)],
            y_s.at[p], y_r.at[p], p,
        )

    for m in (2, 1, 3, 0):
        part = y_peer(m)

        @pl.loop(0, 8)
        def _(i):
            b = part * 8 + i
            acc = hub_acc[:, pl.ds(pl.multiple_of(b * 128, 128), 128)]
            for t in range(4):
                acc = acc + dot(recv[sm[b * 4 + t]], tv[b * 4 + t], NT)
            agg_send[part, :, pl.ds(pl.multiple_of(i * 128, 128), 128)] = acc.astype(BF16)

        if m:
            agg_out(m).start()
    agg_full[pl.ds(pl.multiple_of(y * 64, 64), 64), :] = agg_send[y]
    for m in range(1, 4):
        cot_in(m).wait_recv()
    for m in range(1, 4):
        agg_in(m).wait_recv()

    def ga_out(m, half):
        p = y_peer(m)
        return to_feat(
            gas.at[pl.ds(pl.multiple_of(p * 64, 64), 64), pl.ds(half * 512, 512)],
            ga.at[:, pl.ds(pl.multiple_of(y * 1024 + half * 512, 512), 512)],
            g_s.at[half * 4 + p], g_r.at[half * 4 + y], p,
        )

    def ga_in(m, half):
        p = y_peer(m)
        return to_feat(
            gas.at[pl.ds(pl.multiple_of(p * 64, 64), 64), pl.ds(half * 512, 512)],
            ga.at[:, pl.ds(pl.multiple_of(p * 1024 + half * 512, 512), 512)],
            g_s.at[half * 4 + p], g_r.at[half * 4 + p], p,
        )

    for half in range(2):
        at = pl.ds(half * 512, 512)
        pre = dot(weight[...], agg_full[:, at], TN)
        sigma = jax.nn.sigmoid(pre)
        outs[:, at] = (pre * sigma).astype(BF16)
        slope = (cot_full[:, at].astype(F32) * (sigma * (1.0 + pre * (1.0 - sigma)))).astype(BF16)
        slopes[:, at] = slope
        gas[:, at] = dot(weight[...], slope).astype(BF16)
        for m in (2, 1, 3):
            ga_out(m, half).start()
        ga[:, pl.ds(pl.multiple_of(y * 1024 + half * 512, 512), 512)] = gas[
            pl.ds(pl.multiple_of(y * 64, 64), 64), at
        ]

    for e, m in enumerate((0, 1, 3, 2)):
        part = y_peer(m)
        if m:
            for half in range(2):
                ga_in(m, half).wait_recv()

        @pl.loop(0, 8)
        def _(i):
            b = part * 8 + i
            block = ga[:, pl.ds(pl.multiple_of(b * 128, 128), 128)]
            for t in range(4):
                k = e * 32 + i * 4 + t
                chain[k + 1] = dot(block, tv[b * 4 + t]) + chain[sm[128 + k]]

    def backward(k):
        p = dest(k)
        return to_rows(bsend.at[p], brecv.at[me], b_s.at[p], b_r.at[me], p)

    @pl.loop(0, 63)
    def _(k):
        p = dest(k)
        bsend[p] = chain[sm[256 + p]].astype(BF16)
        backward(k).start()

    brecv[me] = chain[sm[256 + me]].astype(BF16)

    def w_out(m):
        p = y_peer(m)
        return to_feat(
            wt.at[pl.ds(pl.multiple_of(p * 64, 64), 64)], w_y.at[y], wy_s.at[p], wy_r.at[y], p
        )

    def w_in(m):
        p = y_peer(m)
        return to_feat(
            wt.at[pl.ds(pl.multiple_of(p * 64, 64), 64)], w_y.at[p], wy_s.at[p], wy_r.at[p], p
        )

    wt[...] = dot(slopes[...], agg_full[...], NT)
    for m in (2, 1, 3):
        w_out(m).start()
    w_y[y] = wt[pl.ds(pl.multiple_of(y * 64, 64), 64), :]

    def out_out(m):
        p = y_peer(m)
        return to_feat(
            outs.at[pl.ds(pl.multiple_of(p * 64, 64), 64)],
            out.at[:, pl.ds(pl.multiple_of(y * 1024, 1024), 1024)], o_s.at[p], o_r.at[y], p,
        )

    def out_in(m):
        p = y_peer(m)
        return to_feat(
            outs.at[pl.ds(pl.multiple_of(p * 64, 64), 64)],
            out.at[:, pl.ds(pl.multiple_of(p * 1024, 1024), 1024)], o_s.at[p], o_r.at[p], p,
        )

    for m in (2, 1, 3):
        out_out(m).start()
    out[:, pl.ds(pl.multiple_of(y * 1024, 1024), 1024)] = outs[
        pl.ds(pl.multiple_of(y * 64, 64), 64), :
    ]

    terms = dot(ga[...], hadj[...])
    packed = jnp.concatenate([terms[:, :256], terms[:, 256:]], axis=0).T
    for zz in range(4):
        for p in range(8):
            h_1[p, pl.ds(zz * 8, 8), :] = packed[zz * 64 + p * 8 : zz * 64 + p * 8 + 8]

    def h1_out(m):
        p = xc_peer(m)
        return to_rows(h_1.at[p], h_xc.at[xc], h1_s.at[p], h1_r.at[xc], z * 8 + p)

    def h1_in(m):
        p = xc_peer(m)
        return to_rows(h_1.at[p], h_xc.at[p], h1_s.at[p], h1_r.at[p], z * 8 + p)

    @pl.loop(1, 8)
    def _(m):
        h1_out(m).start()

    h_xc[xc] = h_1[xc]

    for m in range(1, 4):
        w_in(m).wait_recv()
    w_1[...] = (w_y[0] + w_y[1] + w_y[2] + w_y[3]).reshape(8, 8, 256)

    def wx_out(m):
        p = xc_peer(m)
        return to_rows(w_1.at[p], w_xc.at[xc], wx_s.at[p], wx_r.at[xc], z * 8 + p)

    def wx_in(m):
        p = xc_peer(m)
        return to_rows(w_1.at[p], w_xc.at[p], wx_s.at[p], wx_r.at[p], z * 8 + p)

    @pl.loop(1, 8)
    def _(m):
        wx_out(m).start()

    w_xc[xc] = w_1[xc]

    def scatter(g):
        q = [source(4 * g + i) for i in range(4)]
        col = jnp.concatenate([cols[pl.ds(p, 1), :] for p in q], axis=1)
        back = jnp.concatenate([brecv[p] for p in q], axis=1).astype(F32)
        high = jnp.broadcast_to(lax.shift_right_arithmetic(col, 9), (64, 512))
        spread = jnp.concatenate(
            [jnp.where(high == hi, back, 0.0).astype(BF16) for hi in range(8)], axis=0
        )
        scat[...] += dot(spread, onehot(col, 512), NT)

    def backward_in(k):
        q = source(k)
        return to_rows(bsend.at[q], brecv.at[q], b_s.at[q], b_r.at[q], q)

    def take(first, last):
        @pl.loop(first, last)
        def _(g):
            for i in range(4):
                backward_in(4 * g + i).wait_recv()
            scatter(g)

    scat[...] = jnp.zeros_like(scat)
    take(0, 2)

    @pl.loop(1, 8)
    def _(m):
        h1_in(m).wait_recv()

    total = h_xc[0]
    for p in range(1, 8):
        total = total + h_xc[p]
    h_2[...] = total.reshape(4, 8, 128)

    def h2_out(m):
        p = z_peer(m)
        return to_rows(h_2.at[lax.rem(p, 4)], h_z.at[z], h2_s.at[p], h2_r.at[z], p * 8 + xc)

    def h2_in(m):
        p = z_peer(m)
        return to_rows(h_2.at[lax.rem(p, 4)], h_z.at[p], h2_s.at[p], h2_r.at[p], p * 8 + xc)

    @pl.loop(1, 8)
    def _(m):
        h2_out(m).start()

    h_z[z] = h_2[lax.rem(z, 4)]

    @pl.loop(1, 8)
    def _(m):
        wx_in(m).wait_recv()

    total = w_xc[0]
    for p in range(1, 8):
        total = total + w_xc[p]
    w_2[...] = total

    def wz_out(m):
        p = z_peer(m)
        return to_rows(w_2, w_z.at[z], wz_s.at[p], wz_r.at[z], p * 8 + xc)

    def wz_in(m):
        p = z_peer(m)
        return to_rows(w_2, w_z.at[p], wz_s.at[p], wz_r.at[p], p * 8 + xc)

    @pl.loop(1, 8)
    def _(m):
        wz_out(m).start()

    w_z[z] = w_2[...]
    take(2, 7)

    @pl.loop(1, 8)
    def _(m):
        wz_in(m).wait_recv()

    total = w_z[0]
    for p in range(1, 8):
        total = total + w_z[p]
    w_3[...] = total

    def w4_out(m):
        p = xc_peer(m)
        return to_rows(w_3, w_4.at[xc], w4_s.at[p], w4_r.at[xc], z * 8 + p)

    def w4_in(m):
        p = xc_peer(m)
        return to_rows(w_3, w_4.at[p], w4_s.at[p], w4_r.at[p], z * 8 + p)

    @pl.loop(1, 8)
    def _(m):
        w4_out(m).start()

    w_4[xc] = w_3[...]

    @pl.loop(1, 8)
    def _(m):
        h2_in(m).wait_recv()

    take(7, 12)

    total = h_z[0]
    for p in range(1, 8):
        total = total + h_z[p]
    hub_grad = jnp.where(jnp.broadcast_to(z, (8, 64)) >= 4, total[:, 64:], total[:, :64])
    coarse = hub_grad.astype(BF16)
    fine = (hub_grad - coarse.astype(F32)).astype(BF16)
    hub16 = jnp.concatenate([coarse.astype(F32), fine.astype(F32)], axis=0).astype(BF16)
    for hi in range(8):
        scat[pl.ds(hi * 64, 64), :] += dot(hub16, onehot_hub[:, pl.ds(hi * 512, 512)], TN)

    @pl.loop(1, 8)
    def _(m):
        w4_in(m).wait_recv()

    gweight[...] = (w_4[...].reshape(64, 256) * (1.0 / math.sqrt(64 * 4096))).T
    for m in range(1, 4):
        out_in(m).wait_recv()

    for m in range(1, 4):
        cot_out(m).wait_send()
        agg_out(m).wait_send()
        ga_out(m, 0).wait_send()
        ga_out(m, 1).wait_send()
        w_out(m).wait_send()
        out_out(m).wait_send()

    @pl.loop(1, 8)
    def _(m):
        hub_stage1(m).wait_send()
        hub_stage2(m).wait_send()
        h1_out(m).wait_send()
        h2_out(m).wait_send()
        wx_out(m).wait_send()
        wz_out(m).wait_send()
        w4_out(m).wait_send()

    @pl.loop(0, 63)
    def _(k):
        forward(k).wait_send()
        backward(k).wait_send()

    take(12, 15)
    for i in range(3):
        backward_in(jnp.int32(60 + i)).wait_recv()
    scatter(jnp.int32(15))
    for hi in range(8):
        gfeats[:, pl.ds(hi * 512, 512)] = scat[pl.ds(hi * 64, 64), :]


def on_device(feats, weight, hub_adj, hub_rows, send_cols, send_counts, tile_cols, tile_vals, cot):
    y = lax.axis_index("feat")
    slot = jnp.arange(128, dtype=jnp.int32)
    cols = jnp.where(slot[None, :] < send_counts[0][:, None], send_cols[0], -1)
    tiles = tile_cols.reshape(128)
    quarter = lax.rem(y + jnp.array([0, 1, 3, 2], jnp.int32), 4)
    worked = tile_cols.reshape(4, 32)[quarter].reshape(128)
    number = slot + 1
    earlier = (worked[None, :] == worked[:, None]) & (slot[None, :] < slot[:, None])
    previous = jnp.max(jnp.where(earlier, number[None, :], 0), axis=1)
    peers = jnp.arange(64, dtype=jnp.int32)
    last = jnp.max(jnp.where(worked[None, :] == peers[:, None], number[None, :], 0), axis=1)
    scalars = jnp.concatenate([tiles, previous, last])
    hubrows = jnp.concatenate([hub_rows, hub_rows]).reshape(16, 1)

    vmem = pl.BlockSpec(memory_space=pltpu.VMEM)
    hbm = pl.BlockSpec(memory_space=pl.ANY)
    smem = pl.BlockSpec(memory_space=pltpu.SMEM)
    dma = lambda n: pltpu.SemaphoreType.DMA((n,))
    out, gfeats, gweight = pl.pallas_call(
        layer_kernel,
        out_shape=(
            jax.ShapeDtypeStruct((64, 4096), BF16),
            jax.ShapeDtypeStruct((64, 4096), F32),
            jax.ShapeDtypeStruct((256, 64), F32),
        ),
        in_specs=[vmem, vmem, hbm, vmem, vmem, hbm, vmem, smem],
        out_specs=(vmem, vmem, vmem),
        scratch_shapes=[
            pltpu.VMEM((4096, 512), BF16),
            pltpu.VMEM((128, 128, 128), BF16),
            pltpu.VMEM((512, 512), BF16),
            pltpu.VMEM((16, 4096), BF16),
            pltpu.VMEM((8, 128), F32),
            pltpu.VMEM((8, 8, 128), F32),
            pltpu.VMEM((64, 128), BF16),
            pltpu.VMEM((8, 64, 128), BF16),
            pltpu.VMEM((512, 128), F32),
            pltpu.VMEM((64, 4096), F32),
            pltpu.VMEM((64, 64, 128), BF16),
            pltpu.VMEM((64, 64, 128), BF16),
            pltpu.VMEM((4, 64, 1024), BF16),
            pltpu.VMEM((256, 1024), BF16),
            pltpu.VMEM((256, 1024), BF16),
            pltpu.VMEM((256, 1024), BF16),
            pltpu.VMEM((256, 1024), BF16),
            pltpu.VMEM((256, 1024), BF16),
            pltpu.VMEM((64, 4096), BF16),
            pltpu.VMEM((129, 64, 128), F32),
            pltpu.VMEM((64, 64, 128), BF16),
            pltpu.VMEM((64, 64, 128), BF16),
            pltpu.VMEM((512, 512), F32),
            pltpu.VMEM((256, 256), F32),
            pltpu.VMEM((4, 64, 256), F32),
            pltpu.VMEM((8, 8, 256), F32),
            pltpu.VMEM((8, 8, 256), F32),
            pltpu.VMEM((8, 256), F32),
            pltpu.VMEM((8, 8, 256), F32),
            pltpu.VMEM((8, 256), F32),
            pltpu.VMEM((8, 8, 256), F32),
            pltpu.VMEM((8, 32, 128), F32),
            pltpu.VMEM((8, 32, 128), F32),
            pltpu.VMEM((4, 8, 128), F32),
            pltpu.VMEM((8, 8, 128), F32),
            dma(2),
            dma(64), dma(64), dma(64), dma(64),
            dma(8), dma(8), dma(8), dma(8),
            dma(4), dma(4), dma(4), dma(4),
            dma(8), dma(8), dma(4), dma(4),
            dma(4), dma(4), dma(8), dma(8), dma(8), dma(8), dma(8), dma(8),
            dma(8), dma(8), dma(8), dma(8),
        ],
        compiler_params=pltpu.CompilerParams(
            collective_id=1, has_side_effects=True, vmem_limit_bytes=48 << 20
        ),
        name="layer",
    )(
        feats, weight, hub_adj, hubrows, cols, tile_vals.reshape(128, 128, 128), cot, scalars,
    )
    return out, gfeats, gweight


def solution(mesh):
    in_specs = (
        P("feat", "rows"),
        P(),
        P("rows", None),
        P("rows"),
        P("rows", None, None),
        P("rows", None),
        P("rows", None),
        P("rows", None, None, None),
        P("feat", "rows"),
    )
    out_specs = (P("feat", "rows"), P("feat", "rows"), P(None, "feat"))
    return jax.shard_map(
        on_device, mesh=mesh, in_specs=in_specs, out_specs=out_specs, check_vma=False
    )
```

time: 485 us -> 107 us (0.22)
  waiting for transfers between devices: 259 us -> 0 us
  Pallas kernels: 0 us -> 96.6 us
  blocking collectives: 67.4 us -> 0 us
  other arithmetic: 53.7 us -> 2.62 us
  local copies, waits for them, and re-layouts: 38 us -> 7.13 us
  matrix products: 27.3 us -> 0 us
  starting transfers between devices: 24 us -> 0 us
  between operations: 14.6 us -> 0.67 us
    unnamed x4 -> x0, waiting for transfers between devices: 177 us -> none
    pallas_call x0 -> x1, Pallas kernels: none -> 96.6 us  [on_device(): pl.pallas_call(layer_kernel, out_shape=(jax.ShapeDtypeStruct((64, 4096),...]
    all_gather x1 -> x0, blocking collectives: 67.4 us -> none  [on_device(): lax.all_gather(own_hubs, 'rows', axis=1, tiled=True)]
    reduce_scatter x1 -> x0, waiting for transfers between devices: 49.4 us -> none  [on_device(): lax.psum_scatter(jnp.dot(own_cols, slope, preferred_element_type=jnp.floa...]
    scatter-add x2 -> x0, other arithmetic: 46.4 us -> none  [the longest x1 45.1 us: on_device(): grad_feats = grad_feats.at[:, flat_cols].add(returned)]
    all_gather x1 -> x0, waiting for transfers between devices: 32.9 us -> none  [on_device(): agg_full = lax.all_gather(agg, 'feat', axis=0, tiled=True)]
    gather x4 -> x1, local copies, waits for them, and re-layouts: 28.4 us -> 0.56 us  [on_device(): worked = tile_cols.reshape(4, 32)[quarter].reshape(128)]
    dot_general x8 -> x0, matrix products: 27.3 us -> none  [the longest x1 4.64 us: on_device(): hub_terms = jnp.dot(grad_agg, hub_adj, preferred_element_type=jnp.float32)]
  transfers between devices with their start and end apart: 5 -> 0, of which waited for: 3 -> 0; matrix products, arithmetic and copies ran while one was open for 2% -> 0% of each run, Pallas kernels for 0% -> 0%
where the time goes in v1:
time: 107 us
  Pallas kernels  96.6 us (90%)
  local copies, waits for them, and re-layouts  7.13 us (7%)
  other arithmetic  2.62 us (2%)
    pallas_call x1, Pallas kernels, on_device(): pl.pallas_call(layer_kernel, out_shape=(jax.ShapeDtypeStruct((64, 4096),...  96.6 us
    unnamed x9, local copies, waits for them, and re-layouts  5.51 us

profile of v1, /device:TPU:1, one launch (start us, length us, event | category | flops | bytes accessed | tf_op | source)
XLA Modules:
  0.0 107.0 jit_solution(8994520664062020012)
XLA Ops:
  0.6 0.7 compare_select_fusion
  1.3 0.8 add_bitcast_fusion
  2.1 0.1 copy.23.hubrows
  2.2 0.8 copy.21
  3.0 0.1 reshape.27
  3.1 0.1 reshape.28
  3.1 0.6 gather_fusion
  3.7 0.1 eq.28
  3.8 0.1 select_reduce_fusion.1
  3.9 0.2 select_reduce_fusion
  4.1 0.8 bitcast_select_fusion.cols
  4.9 0.0 copy-start
  5.0 1.0 copy-done
  6.0 0.0 copy-start.1
  6.0 1.0 copy-done.1
  7.0 0.0 copy-start.2
  7.0 0.9 copy-done.2
  7.9 96.6 %layer.1 = (bf16[64,4096]{1,0:T(8,128)(2,1)S(1)}, f32[64,4096]{1,0:T(8,128)S(1)}, f32[256,64]{1,0:T(8,128)S(1)}) custom-call(bf16[64,4096]{1,0:T(8,128)(2,1)S(1)} %copy-done, bf16[256,256]{1,0:T(8,128)(2,1)S(1)} %copy-done.2, bf16[4096,512]{1,0:T(8,128)(2,1)} %hadj_hbm.1, s32[16,1]{1,0:T(8,128)S(1)} %copy.23.hubrows, s32[64,128]{1,0:T(8,128)S(1)} %bitcast_select_fusion.cols, ...), custom_call_target="tpu_custom_call" | custom-call | tf_op jit(solution)/shard_map/layer/pallas_call | solution.py:547
  104.5 0.7 copy.24
  105.3 0.8 copy.27
  106.0 1.0 copy.28
  (3 shorter events, 0.0 us)
Async XLA Ops:
  4.9 1.0 copy-start
  6.0 1.0 copy-start.1
  7.0 0.9 copy-start.2

commit v2 on v1

v2 whole, which is shorter than its diff:
```python
import functools
import math

import jax
import jax.numpy as jnp
from jax import lax
from jax.experimental import pallas as pl
from jax.experimental.pallas import tpu as pltpu
from jax.sharding import PartitionSpec as P

MESH = pl.DeviceIdType.MESH
F32 = jnp.float32
BF16 = jnp.bfloat16
NN = (((1,), (0,)), ((), ()))
NT = (((1,), (1,)), ((), ()))
TN = (((0,), (0,)), ((), ()))
ORDER = (0, 1, 3, 2)
FORWARD = ((0, 48), (48, 16))
BACKWARD = ((0, 32), (32, 32))
EARLY = 8


def dot(a, b, dims=NN):
    return lax.dot_general(a, b, dims, preferred_element_type=F32)


def layer_kernel(
    feats_hbm, weight_hbm, hadj_hbm, hub_rows_hbm, cols_hbm, counts_hbm, tiles_hbm, tv_hbm, cot_hbm,
    out_hbm, gfeats_hbm, gweight_hbm,
    feats, weight, cot, cols, hub_rows, counts, tiles, links_v, links,
    hadj, tv, feat_hi, onehot_hub, hub_own, hub_z, hub_zb, hub_xc, hub_t, hub_acc,
    send, recv_0, recv_1, agg_0, agg_1, agg_full, cot_full, slopes, outs, gas, ga, chain_0, chain_1,
    bsend, brecv, out, scat, wt, w_y, w_1, w_xc, w_2, w_z, w_3, w_4, w_5, h_1, h_xc, h_2, h_z,
    lsem, a_s, a_r, b_s, b_r0, b_r, hz_s, hz_r, hx_s, hx_r, c_s, c_r, y_s, y_r, g_s, g_r, o_s, o_r,
    wy_s, wy_r, wx_s, wx_r, wz_s, wz_r, w4_s, w4_r, w5_s, w5_r, h1_s, h1_r, h2_s, h2_r,
):
    agg_send = (agg_0, agg_1)
    chain = (chain_0, chain_1)
    recv = (recv_0, recv_1)
    me = lax.axis_index("rows")
    y = lax.axis_index("feat")
    z = lax.div(me, 8)
    xc = lax.rem(me, 8)
    x = lax.div(xc, 2)
    c = lax.rem(xc, 2)

    def dest(k):
        return (
            lax.rem(z + 1 + lax.rem(k, 8), 8) * 8
            + lax.rem(x + 1 + lax.div(k, 16), 4) * 2
            + lax.rem(c + 1 + lax.rem(lax.div(k, 8), 2), 2)
        )

    def source(k):
        return (
            lax.rem(z + 7 - lax.rem(k, 8), 8) * 8
            + lax.rem(x + 3 - lax.div(k, 16), 4) * 2
            + lax.rem(c + 1 + lax.rem(lax.div(k, 8), 2), 2)
        )

    def z_peer(m):
        return lax.rem(z + m, 8)

    def xc_peer(m):
        return lax.rem(xc + m, 8)

    def y_peer(m):
        return lax.rem(y + m, 4)

    def to_rows(src, dst, ssem, rsem, peer):
        return pltpu.make_async_remote_copy(
            src_ref=src, dst_ref=dst, send_sem=ssem, recv_sem=rsem,
            device_id={"rows": peer}, device_id_type=MESH,
        )

    def to_feat(src, dst, ssem, rsem, peer):
        return pltpu.make_async_remote_copy(
            src_ref=src, dst_ref=dst, send_sem=ssem, recv_sem=rsem,
            device_id={"feat": peer}, device_id_type=MESH,
        )

    loads = [
        pltpu.make_async_copy(a, b, lsem.at[i])
        for i, (a, b) in enumerate((
            (feats_hbm, feats), (cols_hbm, cols), (counts_hbm, counts), (hub_rows_hbm, hub_rows),
            (tiles_hbm, tiles), (cot_hbm, cot), (weight_hbm, weight), (hadj_hbm, hadj), (tv_hbm, tv),
        ))
    ]
    for load in loads:
        load.start()
    barrier = pltpu.get_barrier_semaphore()

    @pl.loop(1, 64)
    def _(k):
        pl.semaphore_signal(
            barrier, inc=1, device_id={"rows": lax.rem(me + k, 64)}, device_id_type=MESH
        )

    for m in range(1, 4):
        pl.semaphore_signal(barrier, inc=1, device_id={"feat": y_peer(m)}, device_id_type=MESH)
    for load in loads[:4]:
        load.wait()

    for hi in range(8):
        feat_hi[pl.ds(hi * 64, 64), :] = feats[:, pl.ds(hi * 512, 512)]
    which = lax.rem(lax.broadcasted_iota(jnp.int32, (16, 128), 0), 8)
    hub_row = jnp.zeros((16, 128), jnp.int32)
    for i in range(8):
        hub_row = jnp.where(which == i, hub_rows[i], hub_row)
    for i in range(32):
        at = lax.broadcasted_iota(jnp.int32, (16, 128), 1) + i * 128
        onehot_hub[:, pl.ds(i * 128, 128)] = jnp.where(at == hub_row, 1.0, 0.0).astype(BF16)
    own = dot(onehot_hub[...], feats[...], NT)
    hub_own[...] = jnp.concatenate([own[:8], jnp.zeros((8, 64), F32)], axis=1)
    for part in range(2):
        chain[part][0] = jnp.zeros(chain[part].shape[1:], F32)

    def onehot(col, width):
        low = jnp.broadcast_to(jnp.bitwise_and(col, 511), (512, width))
        at = lax.broadcasted_iota(jnp.int32, (512, width), 0)
        return jnp.where(at == low, 1.0, 0.0).astype(BF16)

    def live(p):
        slot = lax.broadcasted_iota(jnp.int32, (1, 128), 1)
        return jnp.where(slot < counts[0, p], cols[pl.ds(p, 1), :], -1)

    def gather(g):
        p0, p1 = dest(2 * g), dest(2 * g + 1)
        col = jnp.concatenate([live(p0), live(p1)], axis=1)
        picked = dot(feat_hi[...], onehot(col, 256))
        high = jnp.broadcast_to(lax.shift_right_arithmetic(col, 9), (64, 256))
        acc = jnp.zeros((64, 256), F32)
        for hi in range(8):
            acc = jnp.where(high == hi, picked[hi * 64 : hi * 64 + 64], acc)
        acc = acc.astype(BF16)
        send[p0] = acc[:, :128]
        send[p1] = acc[:, 128:]

    def forward(k, part):
        p = dest(k)
        at = pl.ds(*FORWARD[part])
        return to_rows(send.at[p, at], recv[part].at[me], a_s.at[part], a_r.at[part], p)

    def all_forward(sem, part):
        at = recv[part].at[pl.ds(0, 63)]
        return pltpu.make_async_copy(at, at, sem.at[part])

    def all_backward(sem, buf, part):
        at = buf.at[pl.ds(0, 63), pl.ds(*BACKWARD[part])]
        return pltpu.make_async_copy(at, at, sem.at[part])

    @pl.loop(0, EARLY)
    def _(g):
        gather(g)

    pl.semaphore_wait(barrier, 66)

    def hub_stage1(m):
        p = z_peer(m)
        return to_rows(hub_own, hub_z.at[z], hz_s.at[p], hz_r.at[z], p * 8 + xc)

    def hub_stage1_in(m):
        p = z_peer(m)
        return to_rows(hub_own, hub_z.at[p], hz_s.at[p], hz_r.at[p], p * 8 + xc)

    @pl.loop(1, 8)
    def _(m):
        hub_stage1(m).start()

    hub_z[z] = hub_own[...]

    @pl.loop(0, 2 * EARLY)
    def _(k):
        forward(k, 0).start()

    def cot_out(m):
        p = y_peer(m)
        return to_feat(
            cot.at[:, pl.ds(pl.multiple_of(p * 1024, 1024), 1024)],
            cot_full.at[pl.ds(pl.multiple_of(y * 64, 64), 64)], c_s.at[p], c_r.at[y], p,
        )

    def cot_in(m):
        p = y_peer(m)
        return to_feat(
            cot.at[:, pl.ds(pl.multiple_of(p * 1024, 1024), 1024)],
            cot_full.at[pl.ds(pl.multiple_of(p * 64, 64), 64)], c_s.at[p], c_r.at[p], p,
        )

    loads[5].wait()
    for m in (2, 1, 3):
        cot_out(m).start()
    cot_full[pl.ds(pl.multiple_of(y * 64, 64), 64), :] = cot[
        :, pl.ds(pl.multiple_of(y * 1024, 1024), 1024)
    ]

    @pl.loop(EARLY, 31)
    def _(g):
        gather(g)
        forward(2 * g, 0).start()
        forward(2 * g + 1, 0).start()

    gather(jnp.int32(31))
    forward(jnp.int32(62), 0).start()
    for part in range(2):
        recv[part][me] = send[me, pl.ds(*FORWARD[part]), :]

    @pl.loop(0, 63)
    def _(k):
        forward(k, 1).start()

    @pl.loop(1, 8)
    def _(m):
        hub_stage1_in(m).wait_recv()

    hub_zb[...] = hub_z[...].reshape(64, 128).astype(BF16)

    def hub_stage2(m):
        p = xc_peer(m)
        return to_rows(hub_zb, hub_xc.at[xc], hx_s.at[p], hx_r.at[xc], z * 8 + p)

    def hub_stage2_in(m):
        p = xc_peer(m)
        return to_rows(hub_zb, hub_xc.at[p], hx_s.at[p], hx_r.at[p], z * 8 + p)

    @pl.loop(1, 8)
    def _(m):
        hub_stage2(m).start()

    hub_xc[xc] = hub_zb[...]

    loads[4].wait()
    lane = lax.broadcasted_iota(jnp.int32, (1, 128), 1)
    senders = jnp.zeros((1, 128), jnp.int32)
    for e, m in enumerate(ORDER):
        first = y_peer(m) * 8

        def add(i, row):
            for t in range(4):
                row = jnp.where(lane == e * 32 + i * 4 + t, tiles[first + i, t], row)
            return row

        senders = lax.fori_loop(0, 8, add, senders)
    across = jnp.broadcast_to(senders, (128, 128))
    down = across.T
    at_row = lax.broadcasted_iota(jnp.int32, (128, 128), 0)
    at_lane = lax.broadcasted_iota(jnp.int32, (128, 128), 1)
    before = jnp.where(at_row < at_lane, jnp.where(across == down, at_row + 1, 0), 0)
    final = jnp.where(down == at_lane, at_row + 1, 0)
    links_v[...] = jnp.concatenate([
        jnp.max(before, axis=0, keepdims=True), jnp.max(final, axis=0, keepdims=True),
        jnp.zeros((6, 128), jnp.int32),
    ], axis=0)
    fetch = pltpu.make_async_copy(links_v, links, lsem.at[9])
    fetch.start()
    fetch.wait()
    for load in loads[6:]:
        load.wait()

    @pl.loop(1, 8)
    def _(m):
        hub_stage2_in(m).wait_recv()

    for p in range(8):
        part = hub_xc[p].astype(F32)
        for zz in range(8):
            hub_t[pl.ds(zz * 64 + p * 8, 8), :] = part[zz * 8 : zz * 8 + 8]
    hubs = hub_t[...].T[:64].astype(BF16)

    @pl.loop(0, 8)
    def _(n):
        at = pl.ds(pl.multiple_of(n * 512, 512), 512)
        hub_acc[:, at] = dot(hubs, hadj[at, :], NT)

    def agg_move(m, part, slot):
        p = y_peer(m)
        first, count = FORWARD[part]
        return to_feat(
            agg_send[part].at[p],
            agg_full.at[pl.ds(pl.multiple_of(slot * 64 + first, 16), count)],
            y_s.at[part * 4 + p], y_r.at[part * 4 + slot], p,
        )

    def agg_out(m, part):
        return agg_move(m, part, y)

    def agg_in(m, part):
        return agg_move(m, part, y_peer(m))

    def block_tiles(b):
        return jnp.concatenate([tv[b * 4 + t] for t in range(4)], axis=1)

    for part in range(2):
        first, count = FORWARD[part]
        rows = pl.ds(first, count)
        all_forward(a_r, part).wait()
        for m in (2, 1, 3, 0):
            quarter = y_peer(m)

            @pl.loop(0, 8)
            def _(i):
                b = quarter * 8 + i
                listed = jnp.concatenate(
                    [recv[part][tiles[b, t]] for t in range(4)], axis=1
                )
                acc = hub_acc[rows, pl.ds(pl.multiple_of(b * 128, 128), 128)]
                acc = acc + dot(listed, block_tiles(b), NT)
                agg_send[part][quarter, :, pl.ds(pl.multiple_of(i * 128, 128), 128)] = acc.astype(
                    BF16
                )

            if m:
                agg_out(m, part).start()
        agg_full[pl.ds(pl.multiple_of(y * 64 + first, 16), count), :] = agg_send[part][y]
    for m in range(1, 4):
        cot_in(m).wait_recv()
    for part in range(2):
        for m in range(1, 4):
            agg_in(m, part).wait_recv()

    def ga_move(m, part, half, slot):
        p = y_peer(m)
        first, count = BACKWARD[part]
        sem = part * 8 + half * 4
        return to_feat(
            gas.at[pl.ds(pl.multiple_of(p * 64 + first, 16), count), pl.ds(half * 512, 512)],
            ga.at[
                pl.ds(first, count), pl.ds(pl.multiple_of(slot * 1024 + half * 512, 512), 512)
            ],
            g_s.at[sem + p], g_r.at[sem + slot], p,
        )

    def ga_out(m, part, half):
        return ga_move(m, part, half, y)

    def ga_in(m, part, half):
        return ga_move(m, part, half, y_peer(m))

    for half in range(2):
        at = pl.ds(half * 512, 512)
        pre = dot(weight[...], agg_full[:, at], TN)
        sigma = jax.nn.sigmoid(pre)
        outs[:, at] = (pre * sigma).astype(BF16)
        slope = (cot_full[:, at].astype(F32) * (sigma * (1.0 + pre * (1.0 - sigma)))).astype(BF16)
        slopes[:, at] = slope
        gas[:, at] = dot(weight[...], slope).astype(BF16)
        for m in (2, 1, 3):
            ga_out(m, 0, half).start()
        ga[:, pl.ds(pl.multiple_of(y * 1024 + half * 512, 512), 512)] = gas[
            pl.ds(pl.multiple_of(y * 64, 64), 64), at
        ]
    for half in range(2):
        for m in (2, 1, 3):
            ga_out(m, 1, half).start()

    def w_out(m):
        p = y_peer(m)
        return to_feat(
            wt.at[pl.ds(pl.multiple_of(p * 64, 64), 64)], w_y.at[y], wy_s.at[p], wy_r.at[y], p
        )

    def w_in(m):
        p = y_peer(m)
        return to_feat(
            wt.at[pl.ds(pl.multiple_of(p * 64, 64), 64)], w_y.at[p], wy_s.at[p], wy_r.at[p], p
        )

    wt[...] = dot(slopes[...], agg_full[...], NT)
    for m in (2, 1, 3):
        w_out(m).start()
    w_y[y] = wt[pl.ds(pl.multiple_of(y * 64, 64), 64), :]

    def out_out(m):
        p = y_peer(m)
        return to_feat(
            outs.at[pl.ds(pl.multiple_of(p * 64, 64), 64)],
            out.at[:, pl.ds(pl.multiple_of(y * 1024, 1024), 1024)], o_s.at[p], o_r.at[y], p,
        )

    def out_in(m):
        p = y_peer(m)
        return to_feat(
            outs.at[pl.ds(pl.multiple_of(p * 64, 64), 64)],
            out.at[:, pl.ds(pl.multiple_of(p * 1024, 1024), 1024)], o_s.at[p], o_r.at[p], p,
        )

    for m in (2, 1, 3):
        out_out(m).start()
    out[:, pl.ds(pl.multiple_of(y * 1024, 1024), 1024)] = outs[
        pl.ds(pl.multiple_of(y * 64, 64), 64), :
    ]

    def backward(k, part):
        p = dest(k)
        at = pl.ds(*BACKWARD[part])
        rsem = b_r.at[me] if part else b_r0.at[0]
        return to_rows(bsend.at[p, at], brecv.at[me, at], b_s.at[part], rsem, p)

    def tile_products(part):
        first, count = BACKWARD[part]
        for e, m in enumerate(ORDER):
            quarter = y_peer(m)
            if m:
                for half in range(2):
                    ga_in(m, part, half).wait_recv()

            @pl.loop(0, 8)
            def _(i):
                b = quarter * 8 + i
                block = ga[pl.ds(first, count), pl.ds(pl.multiple_of(b * 128, 128), 128)]
                products = dot(block, block_tiles(b))
                for t in range(4):
                    k = e * 32 + i * 4 + t
                    chain[part][k + 1] = (
                        products[:, t * 128 : t * 128 + 128] + chain[part][links[0, k]]
                    )

    def send_back(part):
        first, count = BACKWARD[part]

        @pl.loop(0, 63)
        def _(k):
            p = dest(k)
            bsend[p, pl.ds(first, count), :] = chain[part][links[1, p]].astype(BF16)
            backward(k, part).start()

        brecv[me, pl.ds(first, count), :] = chain[part][links[1, me]].astype(BF16)

    tile_products(0)
    send_back(0)
    tile_products(1)
    terms = dot(ga[...], hadj[...])
    packed = jnp.concatenate([terms[:, :256], terms[:, 256:]], axis=0).T
    for zz in range(4):
        for p in range(8):
            h_1[p, pl.ds(zz * 8, 8), :] = packed[zz * 64 + p * 8 : zz * 64 + p * 8 + 8]

    def h1_out(m):
        p = xc_peer(m)
        return to_rows(h_1.at[p], h_xc.at[xc], h1_s.at[p], h1_r.at[xc], z * 8 + p)

    def h1_in(m):
        p = xc_peer(m)
        return to_rows(h_1.at[p], h_xc.at[p], h1_s.at[p], h1_r.at[p], z * 8 + p)

    @pl.loop(1, 8)
    def _(m):
        h1_out(m).start()

    h_xc[xc] = h_1[xc]

    for m in range(1, 4):
        w_in(m).wait_recv()
    w_1[...] = (w_y[0] + w_y[1] + w_y[2] + w_y[3]).reshape(8, 8, 256)

    def wx_out(m):
        p = xc_peer(m)
        return to_rows(w_1.at[p], w_xc.at[xc], wx_s.at[p], wx_r.at[xc], z * 8 + p)

    def wx_in(m):
        p = xc_peer(m)
        return to_rows(w_1.at[p], w_xc.at[p], wx_s.at[p], wx_r.at[p], z * 8 + p)

    @pl.loop(1, 8)
    def _(m):
        wx_out(m).start()

    w_xc[xc] = w_1[xc]

    send_back(1)

    def scatter(g):
        q = [source(4 * g + i) for i in range(4)]
        col = jnp.concatenate([live(p) for p in q], axis=1)
        back = jnp.concatenate([brecv[p] for p in q], axis=1).astype(F32)
        high = jnp.broadcast_to(lax.shift_right_arithmetic(col, 9), (64, 512))
        spread = jnp.concatenate(
            [jnp.where(high == hi, back, 0.0).astype(BF16) for hi in range(8)], axis=0
        )
        scat[...] += dot(spread, onehot(col, 512), NT)

    def backward_in(k):
        q = source(k)
        at = pl.ds(*BACKWARD[1])
        return to_rows(bsend.at[q, at], brecv.at[q, at], b_s.at[1], b_r.at[q], q)

    def take(first, last):
        @pl.loop(first, last)
        def _(g):
            for i in range(4):
                backward_in(4 * g + i).wait_recv()
            scatter(g)

    scat[...] = jnp.zeros_like(scat)

    @pl.loop(1, 8)
    def _(m):
        h1_in(m).wait_recv()

    total = h_xc[0]
    for p in range(1, 8):
        total = total + h_xc[p]
    h_2[...] = total.reshape(4, 8, 128)

    def h2_out(m):
        p = z_peer(m)
        return to_rows(h_2.at[lax.rem(p, 4)], h_z.at[z], h2_s.at[p], h2_r.at[z], p * 8 + xc)

    def h2_in(m):
        p = z_peer(m)
        return to_rows(h_2.at[lax.rem(p, 4)], h_z.at[p], h2_s.at[p], h2_r.at[p], p * 8 + xc)

    @pl.loop(1, 8)
    def _(m):
        h2_out(m).start()

    h_z[z] = h_2[lax.rem(z, 4)]

    @pl.loop(1, 8)
    def _(m):
        wx_in(m).wait_recv()

    total = w_xc[0]
    for p in range(1, 8):
        total = total + w_xc[p]
    for i in range(8):
        w_2[i] = total[i : i + 1]

    def wz_out(m):
        p = z_peer(m)
        return to_rows(w_2.at[p], w_z.at[z], wz_s.at[p], wz_r.at[z], p * 8 + xc)

    def wz_in(m):
        p = z_peer(m)
        return to_rows(w_2.at[p], w_z.at[p], wz_s.at[p], wz_r.at[p], p * 8 + xc)

    @pl.loop(1, 8)
    def _(m):
        wz_out(m).start()

    w_z[z] = w_2[z]
    all_backward(b_r0, brecv, 0).wait()
    take(0, 4)

    @pl.loop(1, 8)
    def _(m):
        wz_in(m).wait_recv()

    total = w_z[0]
    for p in range(1, 8):
        total = total + w_z[p]
    w_3[...] = total

    def w4_out(m):
        p = z_peer(m)
        return to_rows(w_3, w_4.at[z], w4_s.at[p], w4_r.at[z], p * 8 + xc)

    def w4_in(m):
        p = z_peer(m)
        return to_rows(w_3, w_4.at[p], w4_s.at[p], w4_r.at[p], p * 8 + xc)

    @pl.loop(1, 8)
    def _(m):
        w4_out(m).start()

    w_4[z] = w_3[...]

    @pl.loop(1, 8)
    def _(m):
        h2_in(m).wait_recv()

    take(4, 8)

    @pl.loop(1, 8)
    def _(m):
        w4_in(m).wait_recv()

    def w5_out(m):
        p = xc_peer(m)
        return to_rows(w_4, w_5.at[xc], w5_s.at[p], w5_r.at[xc], z * 8 + p)

    def w5_in(m):
        p = xc_peer(m)
        return to_rows(w_4, w_5.at[p], w5_s.at[p], w5_r.at[p], z * 8 + p)

    @pl.loop(1, 8)
    def _(m):
        w5_out(m).start()

    w_5[xc] = w_4[...]
    take(8, 12)

    total = h_z[0]
    for p in range(1, 8):
        total = total + h_z[p]
    hub_grad = jnp.where(jnp.broadcast_to(z, (8, 64)) >= 4, total[:, 64:], total[:, :64])
    coarse = hub_grad.astype(BF16)
    fine = (hub_grad - coarse.astype(F32)).astype(BF16)
    hub16 = jnp.concatenate([coarse.astype(F32), fine.astype(F32)], axis=0).astype(BF16)
    for hi in range(8):
        scat[pl.ds(hi * 64, 64), :] += dot(hub16, onehot_hub[:, pl.ds(hi * 512, 512)], TN)

    @pl.loop(1, 8)
    def _(m):
        w5_in(m).wait_recv()

    for m in range(1, 4):
        out_in(m).wait_recv()
    stores = [
        pltpu.make_async_copy(out, out_hbm, lsem.at[0]),
        pltpu.make_async_copy(w_5, gweight_hbm, lsem.at[1]),
    ]
    for store in stores:
        store.start()

    for m in range(1, 4):
        cot_out(m).wait_send()
        for part in range(2):
            agg_out(m, part).wait_send()
            ga_out(m, part, 0).wait_send()
            ga_out(m, part, 1).wait_send()
        w_out(m).wait_send()
        out_out(m).wait_send()

    @pl.loop(1, 8)
    def _(m):
        hub_stage1(m).wait_send()
        hub_stage2(m).wait_send()
        h1_out(m).wait_send()
        h2_out(m).wait_send()
        wx_out(m).wait_send()
        wz_out(m).wait_send()
        w4_out(m).wait_send()
        w5_out(m).wait_send()

    for part in range(2):
        all_forward(a_s, part).wait()
    take(12, 15)
    for i in range(3):
        backward_in(jnp.int32(60 + i)).wait_recv()
    scatter(jnp.int32(15))
    for hi in range(8):
        store = pltpu.make_async_copy(
            scat.at[pl.ds(hi * 64, 64)], gfeats_hbm.at[:, pl.ds(hi * 512, 512)], lsem.at[2 + hi]
        )
        store.start()
        stores.append(store)
    for part in range(2):
        all_backward(b_s, bsend, part).wait()
    for store in stores:
        store.wait()


def on_device(feats, weight, hub_adj, hub_rows, send_cols, send_counts, tile_cols, tile_vals, cot):
    hbm = pl.BlockSpec(memory_space=pl.ANY)
    vmem = pltpu.VMEM
    dma = lambda n: pltpu.SemaphoreType.DMA((n,))
    out, gfeats, gweight = pl.pallas_call(
        layer_kernel,
        out_shape=(
            jax.ShapeDtypeStruct((64, 4096), BF16),
            jax.ShapeDtypeStruct((64, 4096), F32),
            jax.ShapeDtypeStruct((8, 8, 1, 256), F32),
        ),
        in_specs=[hbm] * 9,
        out_specs=(hbm,) * 3,
        scratch_shapes=[
            vmem((64, 4096), BF16),
            vmem((256, 256), BF16),
            vmem((64, 4096), BF16),
            vmem((64, 128), jnp.int32),
            pltpu.SMEM((8,), jnp.int32),
            pltpu.SMEM((1, 64), jnp.int32),
            pltpu.SMEM((32, 4), jnp.int32),
            vmem((8, 128), jnp.int32),
            pltpu.SMEM((8, 128), jnp.int32),
            vmem((4096, 512), BF16),
            vmem((128, 128, 128), BF16),
            vmem((512, 512), BF16),
            vmem((16, 4096), BF16),
            vmem((8, 128), F32),
            vmem((8, 8, 128), F32),
            vmem((64, 128), BF16),
            vmem((8, 64, 128), BF16),
            vmem((512, 128), F32),
            vmem((64, 4096), F32),
            vmem((64, 64, 128), BF16),
            vmem((64, FORWARD[0][1], 128), BF16),
            vmem((64, FORWARD[1][1], 128), BF16),
            vmem((4, FORWARD[0][1], 1024), BF16),
            vmem((4, FORWARD[1][1], 1024), BF16),
            vmem((256, 1024), BF16),
            vmem((256, 1024), BF16),
            vmem((256, 1024), BF16),
            vmem((256, 1024), BF16),
            vmem((256, 1024), BF16),
            vmem((64, 4096), BF16),
            vmem((129, BACKWARD[0][1], 128), F32),
            vmem((129, BACKWARD[1][1], 128), F32),
            vmem((64, 64, 128), BF16),
            vmem((64, 64, 128), BF16),
            vmem((64, 4096), BF16),
            vmem((512, 512), F32),
            vmem((256, 256), F32),
            vmem((4, 64, 256), F32),
            vmem((8, 8, 256), F32),
            vmem((8, 8, 256), F32),
            vmem((8, 1, 256), F32),
            vmem((8, 1, 256), F32),
            vmem((1, 256), F32),
            vmem((8, 1, 256), F32),
            vmem((8, 8, 1, 256), F32),
            vmem((8, 32, 128), F32),
            vmem((8, 32, 128), F32),
            vmem((4, 8, 128), F32),
            vmem((8, 8, 128), F32),
            dma(10),
            dma(2), dma(2), dma(2), dma(1), dma(64),
            dma(8), dma(8), dma(8), dma(8),
            dma(4), dma(4), dma(8), dma(8),
            dma(16), dma(16), dma(4), dma(4),
            dma(4), dma(4), dma(8), dma(8), dma(8), dma(8),
            dma(8), dma(8), dma(8), dma(8),
            dma(8), dma(8), dma(8), dma(8),
        ],
        compiler_params=pltpu.CompilerParams(
            collective_id=1, has_side_effects=True, vmem_limit_bytes=60 << 20
        ),
        name="layer",
    )(
        feats, weight, hub_adj, hub_rows, send_cols.reshape(64, 128), send_counts, tile_cols,
        tile_vals.reshape(128, 128, 128), cot,
    )
    grad_weight = gweight.reshape(64, 256).T * (1.0 / math.sqrt(64 * 4096))
    return out, gfeats, grad_weight


def solution(mesh):
    in_specs = (
        P("feat", "rows"),
        P(),
        P("rows", None),
        P("rows"),
        P("rows", None, None),
        P("rows", None),
        P("rows", None),
        P("rows", None, None, None),
        P("feat", "rows"),
    )
    out_specs = (P("feat", "rows"), P("feat", "rows"), P(None, "feat"))
    return jax.shard_map(
        on_device, mesh=mesh, in_specs=in_specs, out_specs=out_specs, check_vma=False
    )
```

time: 107 us -> 99.8 us (0.933)
  Pallas kernels: 96.6 us -> 91.9 us
  other arithmetic: 2.62 us -> 0.9 us
    pallas_call x1, Pallas kernels: 96.6 us -> 91.9 us  [on_device(): pl.pallas_call(layer_kernel, out_shape=(jax.ShapeDtypeStruct((64, 4096),...]
    select_n x2 -> x0, other arithmetic: 1.5 us -> none  [the longest x1 0.83 us: on_device(): cols = jnp.where(slot[None, :] < send_counts[0][:, None], send_cols[0], -1)]
    unnamed x9 -> x4, local copies, waits for them, and re-layouts: 5.51 us -> 6.14 us
where the time goes in v2:
time: 99.8 us; the launch traced here: 99.5 us
  Pallas kernels  91.9 us (92%)
  local copies, waits for them, and re-layouts  6.14 us (6%)
    pallas_call x1, Pallas kernels, on_device(): pl.pallas_call(layer_kernel, out_shape=(jax.ShapeDtypeStruct((64, 4096),...  91.9 us
    unnamed x4, local copies, waits for them, and re-layouts  6.14 us

profile of v2, /device:TPU:1, one launch (start us, length us, event | category | flops | bytes accessed | tf_op | source)
XLA Modules:
  0.0 99.5 jit_solution(9979041562356938407)
XLA Ops:
  0.6 1.4 %copy.12.tiles_hbm = s32[32,4]{1,0:T(8,128)} copy(s32[32,4]{0,1:T(4,128)} %param.15) | data formatting | bytes 1024 | tf_op args[6]
  2.0 91.9 %layer.1 = (bf16[64,4096]{1,0:T(8,128)(2,1)}, f32[64,4096]{1,0:T(8,128)}, f32[8,8,1,256]{3,2,1,0:T(1,128)}) custom-call(bf16[64,4096]{1,0:T(8,128)(2,1)} %feats_hbm.1, bf16[256,256]{1,0:T(8,128)(2,1)} %weight_hbm.1, bf16[4096,512]{1,0:T(8,128)(2,1)} %hadj_hbm.1, s32[8]{0:T(128)} %hub_rows_hbm.1, s32[64,128]{1,0:T(8,128)} %bitcast.9, s32[1,64]{1,0:T(1,128)} %counts_hbm.1, ...), custom_call_target="tpu_custom_call" | custom-call | tf_op jit(solution)/shard_map/layer/pallas_call | solution.py:658
  93.9 0.9 broadcast_multiply_fusion
  94.8 0.6 copy.15
  95.4 1.9 %copy.18 = bf16[64,4096]{1,0:T(8,128)(2,1)} copy(bf16[64,4096]{1,0:T(8,128)(2,1)} %get-tuple-element.12) | data formatting | bytes 1048576
  97.3 2.3 %copy.19 = f32[64,4096]{1,0:T(8,128)} copy(f32[64,4096]{1,0:T(8,128)} %get-tuple-element.13) | data formatting | bytes 2097152
